TPU v7x, 32 devices: a whole 2x2x4 slice. The times are simulated.
32 devices in a mesh: slab: 4 (over z), member: 8 (over y, x, core).
Axes of the slice: x: 2, y: 2, z: 4, core: 2. Of those that a mesh axis runs over, the one named last changes fastest.
Arguments:
- state: float32 [16, 64, 4096], P('member', 'slab'), may hold values from -6 to 6
- winds: float32 [2, 64, 4096], P(None, 'slab'), may hold values from -0.35 to 0.35
- kappa: float32 [64, 4096], P('slab'), may hold values from 0.05 to 0.22
- obs_values: float32 [512, 128], P('slab'), may hold values from -6 to 6
- obs_rinv: float32 [512, 128], P('slab'), may hold values from 0.1 to 1
- owner: int32 [512, 1], P('slab'), may hold values from 0 to 3; in each aligned block of 128 rows (0 to 127, 128 to 255, ...) at most 64 rows name the same one
- obs_rows: int32 [512], P('slab'), may hold values from 0 to 15
- obs_tiles: int32 [512], P('slab'), may hold values from 0 to 31
- counts: int32 [4], P('slab'), may hold values from 64 to 128, as said below
- tile_mask: int32 [4, 32, 32], P('slab'), may hold values 0 or 1
Outputs:
- analysis: float32 [16, 64, 4096], P('member', 'slab')
Inputs may be any that keep to these rules, and one draw needn't show every extreme that they name: Among the 128 profile rows of one slab index at most 64 name the same owner, a bound that some block reaches of them. `counts`: some slab index has all 128 rows live.
All inputs are finite; a program needn't handle non-finite values. No bound on the sum of `tile_mask` on one device may be relied on, other than what follows from the above.
Results may differ from a plain program's by a relative error of at most 0.00011.
Values sent between devices are 32-bit elements; how exact they have to be, the bound alone decides.
A program may use at most 64 MiB of HBM per device.

v0:
```python
import math
import jax
import jax.numpy as jnp
from jax import lax
from jax.sharding import PartitionSpec as P

PROF = 128
FSTEPS = 2
NS_ITERS = 6
HIGHEST_PRECISION = lax.Precision.HIGHEST


def padded(cells, sides, width):
    for axis, dim in sides:
        count = lax.axis_size(axis)
        ends = count - 1
        head = lax.slice_in_dim(cells, 0, width, axis=dim)
        tail = lax.slice_in_dim(cells, cells.shape[dim] - width, cells.shape[dim], axis=dim)
        cells = jnp.concatenate(
            [
                lax.ppermute(tail, axis, [(i, (i + 1) % count) for i in range(ends)]),
                cells,
                lax.ppermute(head, axis, [((i + 1) % count, i) for i in range(ends)]),
            ],
            axis=dim,
        )
    return cells


def step_forward_border(widened_field, coeff_east, coeff_north, diffusion):
    middle_row = widened_field[:, 1:-1]
    northern_row = widened_field[:, 2:]
    southern_row = widened_field[:, :-2]
    eastern_column = jnp.roll(middle_row, -1, 2)
    western_column = jnp.roll(middle_row, 1, 2)
    return (
        middle_row
        - coeff_east * (eastern_column - western_column) * 0.5
        - coeff_north * (northern_row - southern_row) * 0.5
        + diffusion
        * (eastern_column + western_column + northern_row + southern_row - 4.0 * middle_row)
    )


def inverse_root(matrix, order_size):
    identity = jnp.eye(order_size, dtype=jnp.float32)
    frob_norm = jnp.sqrt(jnp.sum(matrix * matrix, axis=(-2, -1), keepdims=True) + 1e-06)
    iterate = matrix / frob_norm
    factor = jnp.broadcast_to(identity, matrix.shape)
    for step_number in range(NS_ITERS):
        middle = 1.5 * identity - 0.5 * jnp.matmul(factor, iterate, precision=HIGHEST_PRECISION)
        iterate = jnp.matmul(iterate, middle, precision=HIGHEST_PRECISION)
        factor = jnp.matmul(middle, factor, precision=HIGHEST_PRECISION)
    return factor / jnp.sqrt(frob_norm)


def weights_for(gram_total, innov_total, members):
    identity = jnp.eye(members, dtype=jnp.float32)
    inv_root = inverse_root(gram_total + (members - 1.0) * identity, members)
    half_step = jnp.einsum("...ij,...j->...i", inv_root, innov_total, precision=HIGHEST_PRECISION)
    mean_shift = jnp.einsum("...ij,...j->...i", inv_root, half_step, precision=HIGHEST_PRECISION)
    return mean_shift[..., :, None] + math.sqrt(members - 1.0) * inv_root


def on_device(
    state, winds, kappa, obs_values, obs_rinv, owner, obs_rows, obs_tiles, counts, tile_mask
):
    lat_rows = state.shape[1]
    predict_members = state
    for step_number in range(FSTEPS):
        widened_field = padded(predict_members, (("slab", 1),), 1)
        predict_members = step_forward_border(widened_field, winds[0], winds[1], kappa)
    cell_major_layout = lax.all_to_all(
        predict_members, "member", split_axis=2, concat_axis=0, tiled=True
    )
    ensemble = cell_major_layout.shape[0]
    cell_width = cell_major_layout.shape[2]
    tiles_here = cell_width // PROF
    ensemble_average = jnp.mean(cell_major_layout, axis=0)
    member_deviation = cell_major_layout - ensemble_average
    slab_count = lax.axis_size("slab")
    per_slab = owner.shape[0]
    first_tile = lax.axis_index("member") * tiles_here
    cells = lat_rows * tiles_here
    tile_off = obs_tiles - first_tile
    inside = (
        (tile_off >= 0)
        & (tile_off < tiles_here)
        & (jnp.arange(per_slab, dtype=jnp.int32) < counts[0])
    )
    target = jnp.where(inside, owner[:, 0] * cells + obs_rows * tiles_here + tile_off, -1)
    placing = (target[None, :] == jnp.arange(slab_count * cells, dtype=jnp.int32)[:, None]).astype(
        jnp.float32
    )
    payload = jnp.concatenate([obs_rinv, obs_rinv * obs_values], axis=1)
    sums = jnp.matmul(placing, payload, precision=HIGHEST_PRECISION)
    sums = lax.all_to_all(
        sums.reshape(slab_count, lat_rows, tiles_here, 2, PROF),
        "slab",
        split_axis=0,
        concat_axis=0,
        tiled=True,
    )
    sums = jnp.sum(sums, axis=0)
    cell_weight, cell_value = (sums[:, :, 0], sums[:, :, 1])
    blocks = member_deviation.reshape(ensemble, lat_rows, tiles_here, PROF)
    mean_blocks = ensemble_average.reshape(lat_rows, tiles_here, PROF)
    gram_here = jnp.einsum(
        "irth,jrth->tij", blocks * cell_weight, blocks, precision=HIGHEST_PRECISION
    )
    innov_here = jnp.einsum(
        "irth,rth->ti", blocks, cell_value - cell_weight * mean_blocks, precision=HIGHEST_PRECISION
    )
    tile_count = tile_mask.shape[1]
    tile_use = jnp.maximum(tile_mask[0].astype(jnp.float32), jnp.eye(tile_count, dtype=jnp.float32))
    use_mine = lax.dynamic_slice_in_dim(tile_use, first_tile, tiles_here, 0)
    gram_next = jnp.einsum(
        "ts,sij->tij",
        use_mine,
        lax.all_gather(gram_here, "member", axis=0, tiled=True),
        precision=HIGHEST_PRECISION,
    )
    innov_next = jnp.einsum(
        "ts,si->ti",
        use_mine,
        lax.all_gather(innov_here, "member", axis=0, tiled=True),
        precision=HIGHEST_PRECISION,
    )
    mixing = weights_for(gram_next, innov_next, ensemble)
    update = jnp.einsum("irth,tij->jrth", blocks, mixing, precision=HIGHEST_PRECISION)
    update = update + ensemble_average.reshape(lat_rows, tiles_here, PROF)
    return lax.all_to_all(
        update.reshape(ensemble, lat_rows, cell_width),
        "member",
        split_axis=0,
        concat_axis=2,
        tiled=True,
    )


def solution(mesh):
    placed = (
        P("member", "slab", None),
        P(None, "slab", None),
        P("slab", None),
        P("slab", None),
        P("slab", None),
        P("slab", None),
        P("slab"),
        P("slab"),
        P("slab"),
        P("slab", None, None),
    )
    return jax.shard_map(
        on_device, mesh=mesh, in_specs=placed, out_specs=P("member", "slab", None), check_vma=False
    )
```

profile of v0, /device:TPU:0, one launch (start us, length us, event | category | flops | bytes accessed | tf_op | source)
XLA Modules:
  0.0 106.8 jit_solution(4325995497282656139)
XLA Ops:
  0.0 1.2 %fusion.48 = (f32[2,1,4096]{2,1,0:T(1,128)S(1)}, f32[2,1,4096]{2,1,0:T(1,128)S(1)}) fusion(f32[2,16,4096]{2,1,0:T(8,128)} %param.10), kind=kLoop, calls=%fused_computation.86 | loop fusion | bytes 131072 | tf_op jit(solution)/shard_map/slice | solution.py:18
  1.2 1.3 %collective-permute-start = (f32[2,1,4096]{2,0,1:T(2,128)S(1)}, f32[2,1,4096]{2,0,1:T(2,128)S(1)}, u32[]{:S(2)}, u32[]{:S(2)}) collective-permute-start(f32[2,1,4096]{2,0,1:T(2,128)S(1)} %copy.153), channel_id=1, source_target_pairs={{8,0},{16,8},{24,16},{9,1},{17,9},{25,17},{10,2},{18,10},{26,18},{... | collective-permute-start | bytes 98312 | tf_op jit(solution)/shard_map/ppermute | solution.py:23
  2.6 5.6 %collective-permute-start.1 = (f32[2,1,4096]{2,0,1:T(2,128)S(1)}, f32[2,1,4096]{2,0,1:T(2,128)S(1)}, u32[]{:S(2)}, u32[]{:S(2)}) collective-permute-start(f32[2,1,4096]{2,0,1:T(2,128)S(1)} %copy.154), channel_id=1, source_target_pairs={{0,8},{8,16},{16,24},{1,9},{9,17},{17,25},{2,10},{10,18},{18,26},{... | collective-permute-start | bytes 98312 | tf_op jit(solution)/shard_map/ppermute | solution.py:21
  8.8 0.9 mul.169
  10.4 1.1 %fusion.14 = f32[256,256]{1,0:T(8,128)S(1)} fusion(f32[128,128]{1,0:T(8,128)S(1)} %mul.169, f32[128,128]{1,0:T(8,128)} %param.14, s32[128]{0:T(128)S(1)} %and_select_fusion), kind=kOutput, calls=%fused_computation.38 | convolution fusion | flops 100728832 | bytes 393728 | tf_op jit(solution)/shard_map/dot_general | solution.py:96
  11.5 0.8 reshape.53
  12.3 4.3 %all-to-all-start.1 = ((f32[4,16,4,2,128]{4,3,2,1,0:T(2,128)}), f32[4,16,4,2,128]{4,3,2,1,0:T(2,128)S(1)}, u32[]{:S(2)}, u32[]{:S(2)}) async-start(f32[4,16,4,2,128]{4,3,2,1,0:T(2,128)} %reshape.53), calls=%async_computation.1 | async-start | bytes 524288 | tf_op jit(solution)/shard_map/all_to_all | solution.py:97
  16.6 1.5 %fusion.46 = (f32[2,16,4095]{2,1,0:T(8,128)S(1)}, f32[2,16,4095]{2,1,0:T(8,128)S(1)}) fusion(f32[2,16,4096]{2,1,0:T(8,128)} %param.10), kind=kLoop, calls=%fused_computation.84 | loop fusion | bytes 2096640 | tf_op jit(solution)/shard_map/jit(_roll_static)/slice | solution.py:34
  19.9 1.3 %collective-permute-start.2 = (f32[2,1,4096]{2,0,1:T(2,128)S(1)}, f32[2,1,4096]{2,0,1:T(2,128)S(1)}, u32[]{:S(2)}, u32[]{:S(2)}) collective-permute-start(f32[2,1,4096]{2,0,1:T(2,128)S(1)} %copy.127), channel_id=1, source_target_pairs={{8,0},{16,8},{24,16},{9,1},{17,9},{25,17},{10,2},{18,10},{26,18},{... | collective-permute-start | bytes 98312 | tf_op jit(solution)/shard_map/ppermute | solution.py:23
  21.2 4.6 %collective-permute-start.3 = (f32[2,1,4096]{2,0,1:T(2,128)S(1)}, f32[2,1,4096]{2,0,1:T(2,128)S(1)}, u32[]{:S(2)}, u32[]{:S(2)}) collective-permute-start(f32[2,1,4096]{2,0,1:T(2,128)S(1)} %copy.129), channel_id=1, source_target_pairs={{0,8},{8,16},{16,24},{1,9},{9,17},{17,25},{2,10},{10,18},{18,26},{... | collective-permute-start | bytes 98312 | tf_op jit(solution)/shard_map/ppermute | solution.py:21
  25.9 1.5 %collective-permute-done.3 = f32[2,1,4096]{2,0,1:T(2,128)S(1)} collective-permute-done((f32[2,1,4096]{2,0,1:T(2,128)S(1)}, f32[2,1,4096]{2,0,1:T(2,128)S(1)}, u32[]{:S(2)}, u32[]{:S(2)}) %collective-permute-start.3) | collective-permute-done | bytes 32800 | tf_op jit(solution)/shard_map/ppermute | solution.py:21
  27.9 4.3 %copy.131 = f32[2,16,4096]{1,0,2:T(2,128)} copy(f32[2,16,4096]{2,1,0:T(8,128)S(1)} %multiply_add_fusion) | data formatting | bytes 1048576 | tf_op jit(solution)/shard_map/add | solution.py:37
  32.2 7.9 %reshape.66 = f32[8,1,16384]{2,1,0:T(1,128)} reshape(f32[4096,2,16]{2,1,0:T(2,128)} %bitcast.106) | data formatting | bytes 1048576
  40.1 3.7 %all-to-all-start = ((f32[8,1,16384]{2,1,0:T(1,128)}), f32[8,1,16384]{2,1,0:T(1,128)S(1)}, u32[]{:S(2)}, u32[]{:S(2)}) async-start(f32[8,1,16384]{2,1,0:T(1,128)} %reshape.66), calls=%async_computation | async-start | bytes 1048576 | tf_op jit(solution)/shard_map/all_to_all | solution.py:73
  44.0 9.5 %all-to-all-done = f32[8,1,16384]{2,1,0:T(1,128)S(1)} async-done(((f32[8,1,16384]{2,1,0:T(1,128)}), f32[8,1,16384]{2,1,0:T(1,128)S(1)}, u32[]{:S(2)}, u32[]{:S(2)}) %all-to-all-start) | async-done | bytes 524320 | tf_op jit(solution)/shard_map/all_to_all | solution.py:73
  54.1 1.9 %reduce.1 = f32[8,16384]{1,0:T(8,128)S(1)} reduce(f32[8,1,16384]{2,1,0:T(1,128)S(1)} %all-to-all-done, f32[]{:T(128)} %broadcast.96), dimensions={1}, to_apply=%all_to_all.29.reduce_sub_computation | reduce | bytes 1048580 | tf_op jit(solution)/shard_map/all_to_all | solution.py:73
  56.0 7.5 %reshape.67 = f32[4096,2,16]{2,1,0:T(2,128)} reshape(f32[8,16384]{1,0:T(8,128)S(1)} %reduce.1) | data formatting | bytes 1048576
  63.5 5.1 %copy.132 = f32[2,16,8,512]{3,1,0,2:T(8,128)S(1)} copy(f32[2,16,8,512]{1,0,3,2:T(2,128)} %bitcast.107) | data formatting | bytes 1048576 | tf_op jit(solution)/shard_map/all_to_all | solution.py:73
  68.9 1.1 %convolution_bitcast_fusion.1 = f32[4,16,16]{2,1,0:T(8,128)S(1)} fusion(f32[16,16,4,128]{3,2,1,0:T(4,128)S(1)} %all_to_all.32, f32[16,4,128]{2,0,1:T(8,128)S(1)} %copy.136, f32[16,4,128]{2,0,1:T(8,128)S(1)} %bitcast.110), kind=kOutput, calls=%fused_computation.16 | convolution fusion | flops 25559040 | bytes 593920 | tf_op jit(solution)/shard_map/irth,jrth->tij/dot_general | solution.py:108
  70.0 8.4 %all_gather.6 = f32[32,16,16]{2,1,0:T(8,128)S(1)} all-gather(f32[4,16,16]{2,1,0:T(8,128)S(1)} %convolution_bitcast_fusion.1), channel_id=1, replica_groups=mesh['slab'=4,'member'=8] {'member'}, dimensions={0}, use_global_device_ids=true | all-gather | bytes 36864 | tf_op jit(solution)/shard_map/all_gather | solution.py:120
  81.5 1.0 fusion.8
  82.5 8.9 %all-gather = f32[8,4,16]{2,1,0:T(4,128)S(1)} all-gather(f32[1,4,16]{2,1,0:T(4,128)S(1)} %bitcast.118), channel_id=1, replica_groups=mesh['slab'=4,'member'=8] {'member'}, dimensions={0}, use_global_device_ids=true | all-gather | bytes 2304 | tf_op jit(solution)/shard_map/all_gather | solution.py:126
  92.2 0.9 fusion
  93.7 12.3 %all_to_all.41 = f32[16,16,512]{2,1,0:T(8,128)S(1)} all-to-all(f32[16,16,512]{2,1,0:T(8,128)S(1)} %reshape.54), channel_id=1, replica_groups=mesh['slab'=4,'member'=8] {'member'}, dimensions={0} | all-to-all | bytes 1048576 | tf_op jit(solution)/shard_map/all_to_all | solution.py:132
  (68 shorter events, 9.2 us)
Async XLA Ops:
  0.0 19.1 %copy-start = (f32[2,16,4096]{2,1,0:T(8,128)S(1)}, f32[2,16,4096]{2,1,0:T(8,128)}, u32[]{:S(2)}) copy-start(f32[2,16,4096]{2,1,0:T(8,128)} %param.10) | copy-start | bytes 1572868
  0.0 18.9 %copy-start.2 = (f32[2,16,4096]{2,1,0:T(8,128)S(1)}, f32[2,16,4096]{2,1,0:T(8,128)}, u32[]{:S(2)}) copy-start(f32[2,16,4096]{2,1,0:T(8,128)} %param.11) | copy-start | bytes 1572868
  0.0 19.1 %copy-start.1 = (f32[16,4096]{1,0:T(8,128)S(1)}, f32[16,4096]{1,0:T(8,128)}, u32[]{:S(2)}) copy-start(f32[16,4096]{1,0:T(8,128)} %param.12) | copy-start | bytes 786436
  1.2 17.8 %collective-permute-start = (f32[2,1,4096]{2,0,1:T(2,128)S(1)}, f32[2,1,4096]{2,0,1:T(2,128)S(1)}, u32[]{:S(2)}, u32[]{:S(2)}) collective-permute-start(f32[2,1,4096]{2,0,1:T(2,128)S(1)} %copy.153), channel_id=1, source_target_pairs={{8,0},{16,8},{24,16},{9,1},{17,9},{25,17},{10,2},{18,10},{26,18},{... | collective-permute-start | bytes 98312 | tf_op jit(solution)/shard_map/ppermute | solution.py:23
  2.6 16.5 %collective-permute-start.1 = (f32[2,1,4096]{2,0,1:T(2,128)S(1)}, f32[2,1,4096]{2,0,1:T(2,128)S(1)}, u32[]{:S(2)}, u32[]{:S(2)}) collective-permute-start(f32[2,1,4096]{2,0,1:T(2,128)S(1)} %copy.154), channel_id=1, source_target_pairs={{0,8},{8,16},{16,24},{1,9},{9,17},{17,25},{2,10},{10,18},{18,26},{... | collective-permute-start | bytes 98312 | tf_op jit(solution)/shard_map/ppermute | solution.py:21
  12.3 27.8 %all-to-all-start.1 = ((f32[4,16,4,2,128]{4,3,2,1,0:T(2,128)}), f32[4,16,4,2,128]{4,3,2,1,0:T(2,128)S(1)}, u32[]{:S(2)}, u32[]{:S(2)}) async-start(f32[4,16,4,2,128]{4,3,2,1,0:T(2,128)} %reshape.53), calls=%async_computation.1 | async-start | bytes 524288 | tf_op jit(solution)/shard_map/all_to_all | solution.py:97
  19.9 6.0 %collective-permute-start.2 = (f32[2,1,4096]{2,0,1:T(2,128)S(1)}, f32[2,1,4096]{2,0,1:T(2,128)S(1)}, u32[]{:S(2)}, u32[]{:S(2)}) collective-permute-start(f32[2,1,4096]{2,0,1:T(2,128)S(1)} %copy.127), channel_id=1, source_target_pairs={{8,0},{16,8},{24,16},{9,1},{17,9},{25,17},{10,2},{18,10},{26,18},{... | collective-permute-start | bytes 98312 | tf_op jit(solution)/shard_map/ppermute | solution.py:23
  21.2 6.1 %collective-permute-start.3 = (f32[2,1,4096]{2,0,1:T(2,128)S(1)}, f32[2,1,4096]{2,0,1:T(2,128)S(1)}, u32[]{:S(2)}, u32[]{:S(2)}) collective-permute-start(f32[2,1,4096]{2,0,1:T(2,128)S(1)} %copy.129), channel_id=1, source_target_pairs={{0,8},{8,16},{16,24},{1,9},{9,17},{17,25},{2,10},{10,18},{18,26},{... | collective-permute-start | bytes 98312 | tf_op jit(solution)/shard_map/ppermute | solution.py:21
  27.8 16.0 %copy-start.3 = (s32[1,32,32]{2,1,0:T(8,128)S(1)}, s32[1,32,32]{2,1,0:T(8,128)}, u32[]{:S(2)}) copy-start(s32[1,32,32]{2,1,0:T(8,128)} %param.19) | copy-start | bytes 12292
  40.1 13.5 %all-to-all-start = ((f32[8,1,16384]{2,1,0:T(1,128)}), f32[8,1,16384]{2,1,0:T(1,128)S(1)}, u32[]{:S(2)}, u32[]{:S(2)}) async-start(f32[8,1,16384]{2,1,0:T(1,128)} %reshape.66), calls=%async_computation | async-start | bytes 1048576 | tf_op jit(solution)/shard_map/all_to_all | solution.py:73
where the time goes:
time: 108 us; the launch traced here: 107 us
  local copies, waits for them, and re-layouts  32 us (30%)
  blocking collectives  29.5 us (27%)
  starting transfers between devices  20.7 us (19%)
  waiting for transfers between devices  11 us (10%)
  matrix products  7.89 us (7%)
  other arithmetic  4.66 us (4%)
  between operations  1.08 us (1%)
    unnamed x12, local copies, waits for them, and re-layouts  15.5 us
    all_to_all x1, blocking collectives, on_device(): lax.all_to_all(update.reshape(ensemble, lat_rows, cell_width), 'member',...  12.3 us
    ppermute x2, starting transfers between devices, padded(): lax.ppermute(tail, axis, [(i, (i + 1) % count) for i in range(ends)])  10.1 us
    all_to_all x1, waiting for transfers between devices, on_device(): lax.all_to_all(predict_members, 'member', split_axis=2, concat_axis=0, ti...  9.52 us
    all_gather x1, blocking collectives, on_device(): lax.all_gather(innov_here, 'member', axis=0, tiled=True)  8.86 us
    all_gather x1, blocking collectives, on_device(): lax.all_gather(gram_here, 'member', axis=0, tiled=True)  8.35 us
    all_to_all x3, local copies, waits for them, and re-layouts, on_device(): lax.all_to_all(predict_members, 'member', split_axis=2, concat_axis=0, ti...  5.82 us
    add x1, local copies, waits for them, and re-layouts, step_forward_border(): middle_row - coeff_east * (eastern_column - western_column) * 0.5  4.34 us
  transfers between devices with their start and end apart: 6, of which 2 were waited for; matrix products, arithmetic and copies ran while one was open for 18% of the time, Pallas kernels for 0%

commit v1 on v0

--- a/solution.py
+++ b/solution.py
@@ -70,8 +70,11 @@
     for step_number in range(FSTEPS):
         widened_field = padded(predict_members, (("slab", 1),), 1)
         predict_members = step_forward_border(widened_field, winds[0], winds[1], kappa)
-    cell_major_layout = lax.all_to_all(
-        predict_members, "member", split_axis=2, concat_axis=0, tiled=True
+    cell_major_layout = jnp.concatenate(
+        lax.all_to_all(
+            jnp.stack(jnp.split(predict_members, lax.axis_size("member"), axis=2)), "member", 0, 0
+        ),
+        axis=0,
     )
     ensemble = cell_major_layout.shape[0]
     cell_width = cell_major_layout.shape[2]

time: 108 us -> 82.8 us (0.77)
  local copies, waits for them, and re-layouts: 32 us -> 11.6 us
  other arithmetic: 4.66 us -> 1.18 us
    unnamed x12 -> x25, local copies, waits for them, and re-layouts: 15.5 us -> 6.76 us
    all_to_all x3 -> x0, local copies, waits for them, and re-layouts: 5.82 us -> none  [on_device(): lax.all_to_all(predict_members, 'member', split_axis=2, concat_axis=0, ti...]
    add x1 -> x0, local copies, waits for them, and re-layouts: 4.34 us -> none  [step_forward_border(): middle_row - coeff_east * (eastern_column - western_column) * 0.5]
    slice x4, local copies, waits for them, and re-layouts: 2.59 us -> 0.55 us  [step_forward_border(): eastern_column = jnp.roll(middle_row, -1, 2)]
    all_to_all x1 -> x0, other arithmetic: 1.88 us -> none  [on_device(): lax.all_to_all(predict_members, 'member', split_axis=2, concat_axis=0, ti...]
  transfers between devices with their start and end apart: 6 -> 6, of which waited for: 2 -> 3; matrix products, arithmetic and copies ran while one was open for 18% -> 10% of each run, Pallas kernels for 0% -> 0%
where the time goes in v1:
time: 82.8 us; the launch traced here: 82.2 us
  blocking collectives  29.5 us (36%)
  starting transfers between devices  20.8 us (25%)
  local copies, waits for them, and re-layouts  11.6 us (14%)
  waiting for transfers between devices  11 us (13%)
  matrix products  7.04 us (9%)
  other arithmetic  1.18 us (1%)
  between operations  1.04 us (1%)
    all_to_all x1, blocking collectives, on_device(): lax.all_to_all(update.reshape(ensemble, lat_rows, cell_width), 'member',...  12.3 us
    ppermute x2, starting transfers between devices, padded(): lax.ppermute(tail, axis, [(i, (i + 1) % count) for i in range(ends)])  10.1 us
    all_to_all x1, waiting for transfers between devices, on_device(): lax.all_to_all(jnp.stack(jnp.split(predict_members, lax.axis_size('member...  9.52 us
    all_gather x1, blocking collectives, on_device(): lax.all_gather(innov_here, 'member', axis=0, tiled=True)  8.85 us
    all_gather x1, blocking collectives, on_device(): lax.all_gather(gram_here, 'member', axis=0, tiled=True)  8.35 us
    unnamed x25, local copies, waits for them, and re-layouts  6.76 us
    all_to_all x1, starting transfers between devices, on_device(): lax.all_to_all(sums.reshape(slab_count, lat_rows, tiles_here, 2, PROF), '...  4.3 us
    all_to_all x1, starting transfers between devices, on_device(): lax.all_to_all(jnp.stack(jnp.split(predict_members, lax.axis_size('member...  3.85 us
  transfers between devices with their start and end apart: 6, of which 3 were waited for; matrix products, arithmetic and copies ran while one was open for 10% of the time, Pallas kernels for 0%

profile of v1, /device:TPU:0, one launch (start us, length us, event | category | flops | bytes accessed | tf_op | source)
XLA Modules:
  0.0 82.2 jit_solution(8541940640679141179)
XLA Ops:
  0.0 1.1 %fusion.56 = (f32[2,1,4096]{2,1,0:T(1,128)S(1)}, f32[2,1,4096]{2,1,0:T(1,128)S(1)}) fusion(f32[2,16,4096]{2,1,0:T(8,128)} %param.10), kind=kLoop, calls=%fused_computation.101 | loop fusion | bytes 131072 | tf_op jit(solution)/shard_map/slice | solution.py:18
  1.1 1.3 %collective-permute-start = (f32[2,1,4096]{2,1,0:T(1,128)S(1)}, f32[2,1,4096]{2,1,0:T(1,128)S(1)}, u32[]{:S(2)}, u32[]{:S(2)}) collective-permute-start(f32[2,1,4096]{2,1,0:T(1,128)S(1)} %get-tuple-element.18), channel_id=1, source_target_pairs={{8,0},{16,8},{24,16},{9,1},{17,9},{25,17},{10,2},{18,10},{26,18},{... | collective-permute-start | bytes 98312 | tf_op jit(solution)/shard_map/ppermute | solution.py:23
  2.4 5.6 %collective-permute-start.1 = (f32[2,1,4096]{2,1,0:T(1,128)S(1)}, f32[2,1,4096]{2,1,0:T(1,128)S(1)}, u32[]{:S(2)}, u32[]{:S(2)}) collective-permute-start(f32[2,1,4096]{2,1,0:T(1,128)S(1)} %get-tuple-element.17), channel_id=1, source_target_pairs={{0,8},{8,16},{16,24},{1,9},{9,17},{17,25},{2,10},{10,18},{18,26},{... | collective-permute-start | bytes 98312 | tf_op jit(solution)/shard_map/ppermute | solution.py:21
  9.7 0.8 reshape.57
  10.5 4.3 %all-to-all-start.1 = ((f32[4,16,4,2,128]{4,3,2,1,0:T(2,128)}), f32[4,16,4,2,128]{4,3,2,1,0:T(2,128)S(1)}, u32[]{:S(2)}, u32[]{:S(2)}) async-start(f32[4,16,4,2,128]{4,3,2,1,0:T(2,128)} %reshape.57), calls=%async_computation.1 | async-start | bytes 524288 | tf_op jit(solution)/shard_map/all_to_all | solution.py:100
  15.1 0.8 copy-done.2
  15.9 0.9 %copy-done.1 = f32[16,4096]{1,0:T(8,128)S(1)} copy-done((f32[16,4096]{1,0:T(8,128)S(1)}, f32[16,4096]{1,0:T(8,128)}, u32[]{:S(2)}) %copy-start.1) | copy-done | bytes 262168
  17.5 1.3 %collective-permute-start.2 = (f32[2,1,4096]{2,1,0:T(1,128)S(1)}, f32[2,1,4096]{2,1,0:T(1,128)S(1)}, u32[]{:S(2)}, u32[]{:S(2)}) collective-permute-start(f32[2,1,4096]{2,1,0:T(1,128)S(1)} %get-tuple-element.10), channel_id=1, source_target_pairs={{8,0},{16,8},{24,16},{9,1},{17,9},{25,17},{10,2},{18,10},{26,18},{... | collective-permute-start | bytes 98312 | tf_op jit(solution)/shard_map/ppermute | solution.py:23
  18.8 4.6 %collective-permute-start.3 = (f32[2,1,4096]{2,1,0:T(1,128)S(1)}, f32[2,1,4096]{2,1,0:T(1,128)S(1)}, u32[]{:S(2)}, u32[]{:S(2)}) collective-permute-start(f32[2,1,4096]{2,1,0:T(1,128)S(1)} %get-tuple-element.9), channel_id=1, source_target_pairs={{0,8},{8,16},{16,24},{1,9},{9,17},{17,25},{2,10},{10,18},{18,26},{... | collective-permute-start | bytes 98312 | tf_op jit(solution)/shard_map/ppermute | solution.py:21
  23.5 1.4 %collective-permute-done.3 = f32[2,1,4096]{2,1,0:T(1,128)S(1)} collective-permute-done((f32[2,1,4096]{2,1,0:T(1,128)S(1)}, f32[2,1,4096]{2,1,0:T(1,128)S(1)}, u32[]{:S(2)}, u32[]{:S(2)}) %collective-permute-start.3) | collective-permute-done | bytes 32800 | tf_op jit(solution)/shard_map/ppermute | solution.py:21
  25.4 0.6 fusion.25
  26.0 0.6 fusion.24
  26.6 0.6 fusion.23
  27.3 0.6 fusion.22
  28.5 0.6 fusion.20
  30.4 3.9 %all-to-all-start = ((f32[8,2,16,512]{3,2,1,0:T(8,128)}), f32[8,2,16,512]{3,2,1,0:T(8,128)S(1)}, u32[]{:S(2)}, u32[]{:S(2)}) async-start(f32[8,2,16,512]{3,2,1,0:T(8,128)} %fusion.18), calls=%async_computation | async-start | bytes 1048576 | tf_op jit(solution)/shard_map/all_to_all | solution.py:74
  34.5 9.5 %all-to-all-done = f32[8,2,16,512]{3,2,1,0:T(8,128)S(1)} async-done(((f32[8,2,16,512]{3,2,1,0:T(8,128)}), f32[8,2,16,512]{3,2,1,0:T(8,128)S(1)}, u32[]{:S(2)}, u32[]{:S(2)}) %all-to-all-start) | async-done | bytes 524320 | tf_op jit(solution)/shard_map/all_to_all | solution.py:74
  44.3 1.1 %convolution_bitcast_fusion.1 = f32[4,16,16]{2,1,0:T(8,128)S(1)} fusion(f32[16,16,4,128]{3,2,1,0:T(4,128)S(1)} %reshape.56, f32[16,4,128]{2,0,1:T(8,128)S(1)} %copy.33, f32[16,4,128]{2,0,1:T(8,128)S(1)} %bitcast.134), kind=kOutput, calls=%fused_computation.16 | convolution fusion | flops 25559040 | bytes 593920 | tf_op jit(solution)/shard_map/irth,jrth->tij/dot_general | solution.py:111
  45.4 8.4 %all_gather.6 = f32[32,16,16]{2,1,0:T(8,128)S(1)} all-gather(f32[4,16,16]{2,1,0:T(8,128)S(1)} %convolution_bitcast_fusion.1), channel_id=1, replica_groups=mesh['slab'=4,'member'=8] {'member'}, dimensions={0}, use_global_device_ids=true | all-gather | bytes 36864 | tf_op jit(solution)/shard_map/all_gather | solution.py:123
  56.9 1.0 %fusion.8 = f32[4,1,16,1]{2,1,3,0:T(1,128)S(1)} fusion(f32[16,16,4,128]{3,2,1,0:T(4,128)S(1)} %reshape.56, f32[16,4,128]{2,0,1:T(8,128)S(1)} %bitcast.135, f32[16,4,128,1]{2,1,0,3:T(4,128)S(1)} %subtract_bitcast_fusion), kind=kOutput, calls=%fused_computation.30 | convolution fusion | flops 1703936 | bytes 590080 | tf_op jit(solution)/shard_map/irth,rth->ti/dot_general | solution.py:114
  57.9 8.9 %all-gather = f32[8,4,16]{2,1,0:T(4,128)S(1)} all-gather(f32[1,4,16]{2,1,0:T(4,128)S(1)} %bitcast.142), channel_id=1, replica_groups=mesh['slab'=4,'member'=8] {'member'}, dimensions={0}, use_global_device_ids=true | all-gather | bytes 2304 | tf_op jit(solution)/shard_map/all_gather | solution.py:129
  67.6 0.9 %fusion = f32[16,16,4,128]{3,0,1,2:T(8,128)S(1)} fusion(f32[16,16,4,128]{3,2,1,0:T(4,128)S(1)} %reshape.56, f32[16,4,128]{2,0,1:T(8,128)S(1)} %bitcast.136, f32[4,16,16]{2,1,0:T(8,128)S(1)} %convolution_divide_fusion, f32[4,16]{1,0:T(4,128)S(1)} %bitcast.141), kind=kOutput, calls=%fused_computation.1 | convolution fusion | flops 25430016 | bytes 1085696 | tf_op jit(solution)/shard_map/irth,tij->jrth/dot_general | solution.py:133
  69.1 12.3 %all_to_all.28 = f32[16,16,512]{2,1,0:T(8,128)S(1)} all-to-all(f32[16,16,512]{2,1,0:T(8,128)S(1)} %reshape.58), channel_id=1, replica_groups=mesh['slab'=4,'member'=8] {'member'}, dimensions={0} | all-to-all | bytes 1048576 | tf_op jit(solution)/shard_map/all_to_all | solution.py:135
  81.4 0.8 %copy.52 = f32[8,2,2,8,512]{4,3,0,2,1:T(8,128)} copy(f32[8,2,2,8,512]{4,3,2,1,0:T(8,128)S(1)} %bitcast.133) | data formatting | bytes 1048576 | tf_op jit(solution)/shard_map/all_to_all | solution.py:135
  (72 shorter events, 9.3 us)
Async XLA Ops:
  0.0 8.6 %copy-start.4 = (f32[128,128]{1,0:T(8,128)S(1)}, f32[128,128]{1,0:T(8,128)}, u32[]{:S(2)}) copy-start(f32[128,128]{1,0:T(8,128)} %param.13) | copy-start | bytes 196612
  0.0 8.6 %copy-start.3 = (f32[128,128]{1,0:T(8,128)S(1)}, f32[128,128]{1,0:T(8,128)}, u32[]{:S(2)}) copy-start(f32[128,128]{1,0:T(8,128)} %param.14) | copy-start | bytes 196612
  1.1 14.8 %collective-permute-start = (f32[2,1,4096]{2,1,0:T(1,128)S(1)}, f32[2,1,4096]{2,1,0:T(1,128)S(1)}, u32[]{:S(2)}, u32[]{:S(2)}) collective-permute-start(f32[2,1,4096]{2,1,0:T(1,128)S(1)} %get-tuple-element.18), channel_id=1, source_target_pairs={{8,0},{16,8},{24,16},{9,1},{17,9},{25,17},{10,2},{18,10},{26,18},{... | collective-permute-start | bytes 98312 | tf_op jit(solution)/shard_map/ppermute | solution.py:23
  2.4 13.5 %collective-permute-start.1 = (f32[2,1,4096]{2,1,0:T(1,128)S(1)}, f32[2,1,4096]{2,1,0:T(1,128)S(1)}, u32[]{:S(2)}, u32[]{:S(2)}) collective-permute-start(f32[2,1,4096]{2,1,0:T(1,128)S(1)} %get-tuple-element.17), channel_id=1, source_target_pairs={{0,8},{8,16},{16,24},{1,9},{9,17},{17,25},{2,10},{10,18},{18,26},{... | collective-permute-start | bytes 98312 | tf_op jit(solution)/shard_map/ppermute | solution.py:21
  8.7 0.7 copy-start.6
  8.7 0.7 copy-start.7
  8.7 0.7 copy-start.8
  9.6 5.1 %copy-start = (f32[2,16,4096]{2,1,0:T(8,128)S(1)}, f32[2,16,4096]{2,1,0:T(8,128)}, u32[]{:S(2)}) copy-start(f32[2,16,4096]{2,1,0:T(8,128)} %param.10) | copy-start | bytes 1572868
  10.5 20.0 %all-to-all-start.1 = ((f32[4,16,4,2,128]{4,3,2,1,0:T(2,128)}), f32[4,16,4,2,128]{4,3,2,1,0:T(2,128)S(1)}, u32[]{:S(2)}, u32[]{:S(2)}) async-start(f32[4,16,4,2,128]{4,3,2,1,0:T(2,128)} %reshape.57), calls=%async_computation.1 | async-start | bytes 524288 | tf_op jit(solution)/shard_map/all_to_all | solution.py:100
  14.8 1.0 %copy-start.2 = (f32[2,16,4096]{2,1,0:T(8,128)S(1)}, f32[2,16,4096]{2,1,0:T(8,128)}, u32[]{:S(2)}) copy-start(f32[2,16,4096]{2,1,0:T(8,128)} %param.11) | copy-start | bytes 1572868
  15.8 0.9 %copy-start.1 = (f32[16,4096]{1,0:T(8,128)S(1)}, f32[16,4096]{1,0:T(8,128)}, u32[]{:S(2)}) copy-start(f32[16,4096]{1,0:T(8,128)} %param.12) | copy-start | bytes 786436
  17.5 6.0 %collective-permute-start.2 = (f32[2,1,4096]{2,1,0:T(1,128)S(1)}, f32[2,1,4096]{2,1,0:T(1,128)S(1)}, u32[]{:S(2)}, u32[]{:S(2)}) collective-permute-start(f32[2,1,4096]{2,1,0:T(1,128)S(1)} %get-tuple-element.10), channel_id=1, source_target_pairs={{8,0},{16,8},{24,16},{9,1},{17,9},{25,17},{10,2},{18,10},{26,18},{... | collective-permute-start | bytes 98312 | tf_op jit(solution)/shard_map/ppermute | solution.py:23
  18.8 6.1 %collective-permute-start.3 = (f32[2,1,4096]{2,1,0:T(1,128)S(1)}, f32[2,1,4096]{2,1,0:T(1,128)S(1)}, u32[]{:S(2)}, u32[]{:S(2)}) collective-permute-start(f32[2,1,4096]{2,1,0:T(1,128)S(1)} %get-tuple-element.9), channel_id=1, source_target_pairs={{0,8},{8,16},{16,24},{1,9},{9,17},{17,25},{2,10},{10,18},{18,26},{... | collective-permute-start | bytes 98312 | tf_op jit(solution)/shard_map/ppermute | solution.py:21
  30.4 3.9 %copy-start.5 = (s32[1,32,32]{2,1,0:T(8,128)S(1)}, s32[1,32,32]{2,1,0:T(8,128)}, u32[]{:S(2)}) copy-start(s32[1,32,32]{2,1,0:T(8,128)} %param.19) | copy-start | bytes 12292
  30.4 13.6 %all-to-all-start = ((f32[8,2,16,512]{3,2,1,0:T(8,128)}), f32[8,2,16,512]{3,2,1,0:T(8,128)S(1)}, u32[]{:S(2)}, u32[]{:S(2)}) async-start(f32[8,2,16,512]{3,2,1,0:T(8,128)} %fusion.18), calls=%async_computation | async-start | bytes 1048576 | tf_op jit(solution)/shard_map/all_to_all | solution.py:74
